TPU v7x, 32 devices: a whole 2x2x4 slice. The times are simulated.
32 devices in a mesh: context: 4 (over y, x), expert: 8 (over z, core).
Axes of the slice: x: 2, y: 2, z: 4, core: 2. Of those that a mesh axis runs over, the one named last changes fastest.
Arguments:
- queries: bfloat16 [64, 3072], P(None, 'expert'), may hold values from -14 to 14
- key_lift: bfloat16 [16, 128, 512], P('expert'), may hold values from -0.5 to 0.5
- value_lift: bfloat16 [16, 512, 128], P('expert'), may hold values from -0.25 to 0.25
- page_pool: bfloat16 [16, 64, 576], P('context'), may hold values from -6 to 6
- fresh_latents: bfloat16 [8, 8, 576], P('context'), may hold values from -6 to 6
- page_table: int32 [8, 12], replicated, may hold values from 0 to 15, as said below
- context_lengths: int32 [8], replicated, may hold values from 705 to 768, as said below
- tree_parents: int32 [8, 8], replicated, may hold values from -1 to 6, as said below
- out_weight: bfloat16 [2048, 7168], P('expert', 'context'), may hold values from -0.5 to 0.5
- residual: bfloat16 [64, 7168], P('expert', 'context'), may hold values from -6 to 6
- norm_gain: float32 [7168], replicated, may hold values from 0.5 to 2
- expert_ids: int32 [64, 8], P('expert'), may hold values from 0 to 7, all different within a row; in each aligned block of 8 rows (0 to 7, 8 to 15, ...) at most 8 rows name the same one
- route_weights: float32 [64, 8], P('expert'), may hold values from 0.1 to 0.6
- gate_matrix: bfloat16 [8, 7168, 1024], P('expert', None, 'context'), may hold values from -0.0625 to 0.0625
- up_matrix: bfloat16 [8, 7168, 1024], P('expert', None, 'context'), may hold values from -0.0625 to 0.0625
- down_matrix: bfloat16 [8, 1024, 7168], P('expert', 'context'), may hold values from -0.1875 to 0.1875
Outputs:
- layer_out: bfloat16 [64, 7168], P('expert', 'context')
Inputs may be any that keep to these rules, and one draw needn't show every extreme that they name: `page_table`: the 12 pages of a leaf are distinct. `context_lengths`: entry k of a leaf's page table holds its context tokens k * 64 to k * 64 + 63; some leaf fills all 12 pages. `tree_parents`: token 0 of a leaf has parent -1; token t > 0 has a parent among tokens 0 to t - 1 of the same leaf. `expert_ids`: within each aligned block of 8 rows, no expert is named by more than 8 rows, a bound that some block reaches.
All inputs are finite; a program needn't handle non-finite values.
Results may differ from a plain program's by a relative error of at most 0.011.
Values may be sent and summed in bfloat16 or wider, within the bound.
A program may use at most 64 MiB of HBM per device.

v0:
```python
import jax
import jax.numpy as jnp
from jax import lax
from jax.sharding import PartitionSpec as P

LAT = 512
ROPE = 64
QK = 128


NEGATIVE_FILL = -1e30
NORM_EPSILON = 1e-06


def ancestry(tree_parents):
    advance = tree_parents.shape[1]
    positions = jnp.arange(advance, dtype=jnp.int32)
    current = jnp.broadcast_to(positions[None, :], tree_parents.shape)
    linked = current[:, :, None] == positions[None, None, :]
    for repeat in range(advance - 1):
        climbed = jnp.take_along_axis(tree_parents, jnp.maximum(current, 0), axis=1)
        current = jnp.where(current >= 0, climbed, -1)
        linked = linked | (current[:, :, None] == positions[None, None, :])
    return linked


def page_limits(page_table, context_lengths, first_page, page_count, page_len):
    page_ids = first_page + jnp.arange(page_count, dtype=jnp.int32)
    matches = page_table[:, :, None] == page_ids[None, None, :]
    offsets = jnp.arange(page_table.shape[1], dtype=jnp.int32) * page_len
    remain = context_lengths[:, None] - offsets[None, :]
    return jnp.sum(jnp.where(matches, remain[:, :, None], 0), axis=1)


def context_mask(limits, page_len, advance):
    within = jnp.arange(page_len, dtype=jnp.int32)
    visible = within[None, None, :] < limits[:, :, None]
    visible = visible.reshape(limits.shape[0], -1)
    return jnp.repeat(visible, advance, axis=0)


def normalize(values, norm_gain):
    floats = values.astype(jnp.float32)
    inverse = lax.rsqrt(jnp.mean(floats * floats, axis=-1, keepdims=True) + NORM_EPSILON)
    return (floats * inverse * norm_gain).astype(jnp.bfloat16)


def absorbed_queries(queries, key_lift):
    head_count = key_lift.shape[0]
    shaped = queries.reshape(queries.shape[0], head_count, QK + ROPE)
    latent = jnp.einsum(
        "rhq,hql->rhl", shaped[:, :, :QK], key_lift, preferred_element_type=jnp.float32
    ).astype(jnp.bfloat16)
    return jnp.concatenate([latent, shaped[:, :, QK:]], axis=2)


def score_parts(joined_query, pool_keys, row_mask, fresh_keys, fresh_mask, row_start):
    score_scale = (QK + ROPE) ** (-0.5)
    flat_keys = pool_keys.reshape(-1, pool_keys.shape[-1])
    page_scores = (
        jnp.einsum("rhc,kc->rhk", joined_query, flat_keys, preferred_element_type=jnp.float32)
        * score_scale
    )
    page_scores = jnp.where(row_mask[:, None, :], page_scores, NEGATIVE_FILL)
    leaf_count, advance = (fresh_keys.shape[0], fresh_keys.shape[1])
    own_rows = lax.dynamic_slice_in_dim(joined_query, row_start, leaf_count * advance, 0)
    own_rows = own_rows.reshape(leaf_count, advance, joined_query.shape[1], joined_query.shape[2])
    fresh_scores = (
        jnp.einsum("lthc,lsc->lths", own_rows, fresh_keys, preferred_element_type=jnp.float32)
        * score_scale
    )
    fresh_scores = jnp.where(fresh_mask[:, :, None, :], fresh_scores, NEGATIVE_FILL)
    return (page_scores, fresh_scores)


def local_maximum(page_scores, fresh_scores, row_start):
    page_best = jnp.max(page_scores, axis=2)
    fresh_best = jnp.max(fresh_scores, axis=3).reshape(-1, page_scores.shape[1])
    current = lax.dynamic_slice_in_dim(page_best, row_start, fresh_best.shape[0], 0)
    return lax.dynamic_update_slice_in_dim(
        page_best, jnp.maximum(current, fresh_best), row_start, 0
    )


def weighted_sums(page_scores, fresh_scores, row_max, pool_keys, fresh_keys, row_start):
    page_exp = jnp.exp(page_scores - row_max[:, :, None])
    flat_keys = pool_keys.reshape(-1, pool_keys.shape[-1])[:, :LAT]
    totals = jnp.sum(page_exp, axis=2)
    numerators = jnp.einsum(
        "rhk,kl->rhl", page_exp.astype(jnp.bfloat16), flat_keys, preferred_element_type=jnp.float32
    )
    leaf_count, advance = (fresh_keys.shape[0], fresh_keys.shape[1])
    count_rows = leaf_count * advance
    head_count = row_max.shape[1]
    own_max = lax.dynamic_slice_in_dim(row_max, row_start, count_rows, 0).reshape(
        leaf_count, advance, head_count
    )
    fresh_exp = jnp.exp(fresh_scores - own_max[:, :, :, None])
    fresh_totals = jnp.sum(fresh_exp, axis=3).reshape(count_rows, head_count)
    fresh_numer = jnp.einsum(
        "lths,lsc->lthc",
        fresh_exp.astype(jnp.bfloat16),
        fresh_keys[:, :, :LAT],
        preferred_element_type=jnp.float32,
    )
    fresh_numer = fresh_numer.reshape(count_rows, head_count, LAT)
    totals = lax.dynamic_update_slice_in_dim(
        totals,
        lax.dynamic_slice_in_dim(totals, row_start, count_rows, 0) + fresh_totals,
        row_start,
        0,
    )
    numerators = lax.dynamic_update_slice_in_dim(
        numerators,
        lax.dynamic_slice_in_dim(numerators, row_start, count_rows, 0) + fresh_numer,
        row_start,
        0,
    )
    return (totals, numerators)


def project_values(numerators, lift_float):
    return jnp.einsum("rhl,hlv->rhv", numerators, lift_float, precision=lax.Precision.HIGHEST)


def local(
    queries,
    key_lift,
    value_lift,
    page_pool,
    fresh_latents,
    page_table,
    context_lengths,
    tree_parents,
    out_weight,
    residual,
    norm_gain,
    expert_ids,
    route_weights,
    gate_matrix,
    up_matrix,
    down_matrix,
):
    row_total = queries.shape[0]
    advance = tree_parents.shape[1]
    page_len = page_pool.shape[1]
    joined_query = absorbed_queries(queries, key_lift)
    lift_float = value_lift.astype(jnp.float32)
    context_index = lax.axis_index("context")
    leaf_count = fresh_latents.shape[0]
    leaf_start = context_index * leaf_count
    row_start = leaf_start * advance
    own_parents = lax.dynamic_slice_in_dim(tree_parents, leaf_start, leaf_count, 0)
    fresh_mask = ancestry(own_parents)
    limits = page_limits(
        page_table,
        context_lengths,
        context_index * page_pool.shape[0],
        page_pool.shape[0],
        page_len,
    )
    row_mask = context_mask(limits, page_len, advance)
    page_scores, fresh_scores = score_parts(
        joined_query, page_pool, row_mask, fresh_latents, fresh_mask, row_start
    )
    row_max = lax.pmax(local_maximum(page_scores, fresh_scores, row_start), "context")
    totals, numerators = weighted_sums(
        page_scores, fresh_scores, row_max, page_pool, fresh_latents, row_start
    )
    totals, numerators = lax.psum((totals, numerators), "context")
    projected = project_values(numerators, lift_float)
    attention = (projected / totals[:, :, None]).astype(jnp.bfloat16).reshape(row_total, -1)
    row_dev = residual.shape[0]
    head_mix = lax.psum_scatter(
        jnp.dot(attention, out_weight, preferred_element_type=jnp.float32),
        "expert",
        scatter_dimension=0,
        tiled=True,
    )
    hidden_state = (residual.astype(jnp.float32) + head_mix).astype(jnp.bfloat16)
    expert_total = lax.axis_size("expert") * gate_matrix.shape[0]
    top_count = expert_ids.shape[1]
    capacity = max(3, (row_dev * top_count + expert_total - 1) // expert_total)
    flat_ids = expert_ids.reshape(-1)
    onehot = (flat_ids[:, None] == jnp.arange(expert_total, dtype=jnp.int32)[None, :]).astype(
        jnp.int32
    )
    earlier = jnp.cumsum(onehot, axis=0) - onehot
    slot_index = jnp.sum(earlier * onehot, axis=1)
    target = flat_ids * capacity + slot_index
    slot_ids = jnp.arange(expert_total * capacity, dtype=jnp.int32)
    slot_match = target.reshape(row_dev, top_count)[None, :, :] == slot_ids[:, None, None]
    dispatch = jnp.any(slot_match, axis=2).astype(jnp.bfloat16)
    full_rows = lax.all_gather(hidden_state, "context", axis=1, tiled=True)
    normed = normalize(full_rows, norm_gain)
    outgoing = jnp.dot(dispatch, normed, preferred_element_type=jnp.float32).astype(jnp.bfloat16)
    outgoing = outgoing.reshape(expert_total, capacity, -1)
    inputs = lax.all_to_all(outgoing, "expert", split_axis=0, concat_axis=0, tiled=True)
    sources, slots_here, feature_count = inputs.shape
    flat_rows = inputs.reshape(-1, feature_count)
    gate_part = jnp.dot(flat_rows, gate_matrix[0], preferred_element_type=jnp.float32)
    up_part = jnp.dot(flat_rows, up_matrix[0], preferred_element_type=jnp.float32)
    active = (jax.nn.silu(gate_part) * up_part).astype(jnp.bfloat16)
    partial_out = jnp.dot(active, down_matrix[0], preferred_element_type=jnp.float32)
    partial_out = partial_out.reshape(sources, slots_here, feature_count)
    summed = lax.psum_scatter(
        partial_out.astype(jnp.bfloat16), "context", scatter_dimension=2, tiled=True
    )
    returned = lax.all_to_all(summed, "expert", split_axis=0, concat_axis=0, tiled=True)
    slot_rows = returned.reshape(-1, returned.shape[2])
    picked = jnp.take(slot_rows, target, axis=0).reshape(row_dev, top_count, -1).astype(jnp.float32)
    mixed_sum = jnp.sum(route_weights[:, :, None] * picked, axis=1)
    return (hidden_state.astype(jnp.float32) + mixed_sum).astype(jnp.bfloat16)


def solution(mesh):
    return jax.shard_map(
        local,
        mesh=mesh,
        in_specs=(
            P(None, "expert"),
            P("expert", None, None),
            P("expert", None, None),
            P("context", None, None),
            P("context", None, None),
            P(),
            P(),
            P(),
            P("expert", "context"),
            P("expert", "context"),
            P(),
            P("expert", None),
            P("expert", None),
            P("expert", None, "context"),
            P("expert", None, "context"),
            P("expert", "context", None),
        ),
        out_specs=P("expert", "context"),
        check_vma=False,
    )
```

profile of v0, /device:TPU:0, one launch (start us, length us, event | category | flops | bytes accessed | tf_op | source)
XLA Modules:
  0.0 196.9 jit_solution(16796802995426423274)
XLA Ops:
  6.6 1.0 reshape.189
  7.7 0.7 constant_dynamic-slice_fusion.2
  9.3 0.7 gather_fusion.2
  10.2 0.7 gather_fusion.3
  11.1 0.7 gather_fusion.4
  11.9 0.7 gather_fusion.5
  12.8 0.7 gather_fusion.6
  13.7 0.7 gather_fusion.7
  16.2 11.4 %pmax.7 = f32[64,2]{0,1:T(2,128)S(1)} all-reduce(f32[64,2]{0,1:T(2,128)S(1)} %dynamic_update_slice.9), channel_id=1, replica_groups=mesh['context'=4,'expert'=8] {'context'}, use_global_device_ids=true, to_apply=%region_3.5 | all-reduce | flops 128 | bytes 1024 | tf_op jit(solution)/shard_map/pmax | solution.py:166
  28.3 0.7 copy-done.1
  29.5 8.1 %psum.15 = f32[64,2]{0,1:T(2,128)S(1)} all-reduce(f32[64,2]{0,1:T(2,128)S(1)} %dynamic_update_slice.11), channel_id=1, replica_groups=mesh['context'=4,'expert'=8] {'context'}, use_global_device_ids=true, to_apply=%region_7.9 | all-reduce | flops 128 | bytes 1024 | tf_op jit(solution)/shard_map/psum | solution.py:170
  37.5 34.0 %all-reduce.2.cloned.1.call-done = f32[64,2,512]{2,0,1:T(8,128)} async-done(((f32[64,2,512]{2,0,1:T(8,128)}), f32[64,2,512]{2,0,1:T(8,128)}) %all-reduce.2.cloned.1.call-update) | async-done | bytes 262160 | tf_op jit(solution)/shard_map/psum | solution.py:170
  71.5 1.2 fusion.21
  72.8 1.1 fusion.49
  74.5 30.2 %reduce-scatter.3.cloned.1.call-done = f32[8,1792]{1,0:T(8,128)} async-done(((f32[64,1792]{1,0:T(8,128)}), f32[8,1792]{1,0:T(8,128)}) %reduce-scatter.3.cloned.1.call-update) | async-done | bytes 57360 | tf_op jit(solution)/shard_map/reduce_scatter | solution.py:174
  104.8 0.8 add_convert_fusion.1
  105.6 8.4 %all_gather.3 = bf16[8,7168]{1,0:T(8,128)(2,1)S(1)} all-gather(bf16[8,1792]{1,0:T(8,128)(2,1)S(1)} %add_convert_fusion.1), channel_id=1, replica_groups=mesh['context'=4,'expert'=8] {'context'}, dimensions={1}, use_global_device_ids=true | all-gather | bytes 143360 | tf_op jit(solution)/shard_map/all_gather | solution.py:194
  114.7 26.2 %all_to_all.10 = bf16[8,8,7168]{2,1,0:T(8,128)(2,1)S(1)} all-to-all(bf16[8,8,7168]{2,1,0:T(8,128)(2,1)S(1)} %fusion), channel_id=1, replica_groups=mesh['context'=4,'expert'=8] {'expert'}, dimensions={0} | all-to-all | bytes 1835008 | tf_op jit(solution)/shard_map/all_to_all | solution.py:198
  140.9 2.8 %fusion.4 = f32[64,256]{1,0:T(8,128)S(1)} fusion(bf16[1,7168,256]{2,1,0:T(8,128)(2,1)} %param.31, bf16[8,8,7168]{2,1,0:T(8,128)(2,1)S(1)} %all_to_all.10), kind=kOutput, calls=%fused_computation.14 | convolution fusion | flops 234881024 | bytes 4653056 | tf_op jit(solution)/shard_map/dot_general | solution.py:201
  143.6 6.3 %convolution_convert_fusion.1 = bf16[8,8,7168]{2,1,0:T(8,128)(2,1)} fusion(bf16[1,256,7168]{2,1,0:T(8,128)(2,1)} %param.33, bf16[1,7168,256]{2,1,0:T(8,128)(2,1)} %param.32, bf16[8,8,7168]{2,1,0:T(8,128)(2,1)S(1)} %all_to_all.10, f32[64,256]{1,0:T(8,128)S(1)} %fusion.4), kind=kOutput, calls=%fused_computation.9 | convolution fusion | flops 470319104 | bytes 9240576 | tf_op jit(solution)/shard_map/dot_general | solution.py:204
  150.0 25.1 %reduce-scatter.5.cloned.1.call-done = bf16[8,8,1792]{2,1,0:T(8,128)(2,1)} async-done(((bf16[8,8,7168]{2,1,0:T(8,128)(2,1)}), bf16[8,8,1792]{2,1,0:T(8,128)(2,1)}) %reduce-scatter.5.cloned.1.call-update) | async-done | bytes 229392 | tf_op jit(solution)/shard_map/reduce_scatter | solution.py:206
  175.1 4.6 %all-to-all-start.1 = ((bf16[8,8,1792]{2,1,0:T(8,128)(2,1)}), bf16[8,8,1792]{2,1,0:T(8,128)(2,1)S(1)}, u32[]{:S(2)}, u32[]{:S(2)}) async-start(bf16[8,8,1792]{2,1,0:T(8,128)(2,1)} %reduce-scatter.5.cloned.1.call-done), calls=%async_computation.3 | async-start | bytes 458752 | tf_op jit(solution)/shard_map/all_to_all | solution.py:209
  179.8 8.9 %all-to-all-done.1 = bf16[8,8,1792]{2,1,0:T(8,128)(2,1)S(1)} async-done(((bf16[8,8,1792]{2,1,0:T(8,128)(2,1)}), bf16[8,8,1792]{2,1,0:T(8,128)(2,1)S(1)}, u32[]{:S(2)}, u32[]{:S(2)}) %all-to-all-start.1) | async-done | bytes 229408 | tf_op jit(solution)/shard_map/all_to_all | solution.py:209
  188.7 0.7 gather_fusion
  (103 shorter events, 7.1 us)
Async XLA Ops:
  6.5 66.2 %copy-start = (bf16[256,1792]{1,0:T(8,128)(2,1)S(1)}, bf16[256,1792]{1,0:T(8,128)(2,1)}, u32[]{:S(2)}) copy-start(bf16[256,1792]{1,0:T(8,128)(2,1)} %param.26) | copy-start | bytes 2752516
  6.5 65.0 %all-reduce.2.cloned.1.call-start = ((), (), s32[]{:S(2)}) async-start(), calls=%async_computation.4 | async-start | bytes 524288 | tf_op jit(solution)/shard_map/psum | solution.py:170
  8.4 6.1 %copy-start.3 = (bf16[2,128,512]{2,1,0:T(8,128)(2,1)S(1)}, bf16[2,128,512]{2,1,0:T(8,128)(2,1)}, u32[]{:S(2)}) copy-start(bf16[2,128,512]{2,1,0:T(8,128)(2,1)} %param.19) | copy-start | bytes 786436
  9.1 5.6 %copy-start.5 = (bf16[2,8,576]{2,1,0:T(8,128)(2,1)S(1)}, bf16[2,8,576]{2,1,0:T(8,128)(2,1)}, u32[]{:S(2)}) copy-start(bf16[2,8,576]{2,1,0:T(8,128)(2,1)} %param.22) | copy-start | bytes 55300
  9.1 6.0 %copy-start.11 = (s32[8]{0:T(128)S(1)}, s32[8]{0:T(128)}, u32[]{:S(2)}) copy-start(s32[8]{0:T(128)} %param.24) | copy-start | bytes 100
  9.1 6.0 %copy-start.10 = (s32[8,12]{1,0:T(8,128)S(1)}, s32[8,12]{1,0:T(8,128)}, u32[]{:S(2)}) copy-start(s32[8,12]{1,0:T(8,128)} %param.23) | copy-start | bytes 1156
  9.1 6.6 %copy-start.4 = (bf16[4,64,576]{2,1,0:T(8,128)(2,1)S(1)}, bf16[4,64,576]{2,1,0:T(8,128)(2,1)}, u32[]{:S(2)}) copy-start(bf16[4,64,576]{2,1,0:T(8,128)(2,1)} %param.21) | copy-start | bytes 884740
  10.9 60.7 %copy-start.2 = (bf16[2,512,128]{2,1,0:T(8,128)(2,1)S(1)}, bf16[2,512,128]{2,1,0:T(8,128)(2,1)}, u32[]{:S(2)}) copy-start(bf16[2,512,128]{2,1,0:T(8,128)(2,1)} %param.20) | copy-start | bytes 786436
  12.8 61.1 %copy-start.6 = (s32[8,8]{1,0:T(8,128)S(1)}, s32[8,8]{1,0:T(8,128)}, u32[]{:S(2)}) copy-start(s32[8,8]{1,0:T(8,128)} %param.29) | copy-start | bytes 772
  12.8 92.0 %copy-start.7 = (bf16[8,1792]{1,0:T(8,128)(2,1)S(1)}, bf16[8,1792]{1,0:T(8,128)(2,1)}, u32[]{:S(2)}) copy-start(bf16[8,1792]{1,0:T(8,128)(2,1)} %param.27) | copy-start | bytes 86020
  13.5 100.7 %copy-start.8 = (f32[7168]{0:T(1024)S(1)}, f32[7168]{0:T(1024)}, u32[]{:S(2)}) copy-start(f32[7168]{0:T(1024)} %param.28) | copy-start | bytes 86020
  28.3 0.7 copy-start.1
  29.0 75.7 %reduce-scatter.3.cloned.1.call-start = ((), (), s32[]{:S(2)}) async-start(), calls=%async_computation.5 | async-start | bytes 516096 | tf_op jit(solution)/shard_map/reduce_scatter | solution.py:174
  73.8 101.3 %reduce-scatter.5.cloned.1.call-start = ((), (), s32[]{:S(2)}) async-start(), calls=%async_computation.6 | async-start | bytes 1146880 | tf_op jit(solution)/shard_map/reduce_scatter | solution.py:206
  143.6 45.9 %copy-start.9 = (f32[8,8]{1,0:T(8,128)S(1)}, f32[8,8]{1,0:T(8,128)}, u32[]{:S(2)}) copy-start(f32[8,8]{1,0:T(8,128)} %param.30) | copy-start | bytes 772
  175.1 13.6 %all-to-all-start.1 = ((bf16[8,8,1792]{2,1,0:T(8,128)(2,1)}), bf16[8,8,1792]{2,1,0:T(8,128)(2,1)S(1)}, u32[]{:S(2)}, u32[]{:S(2)}) async-start(bf16[8,8,1792]{2,1,0:T(8,128)(2,1)} %reduce-scatter.5.cloned.1.call-done), calls=%async_computation.3 | async-start | bytes 458752 | tf_op jit(solution)/shard_map/all_to_all | solution.py:209
Sparse Core Ops, SparseCore 0:
  29.1 42.3 all-reduce.1
  74.0 30.7 reduce-scatter.2
  150.1 24.9 reduce-scatter.4
where the time goes:
time: 197 us
  waiting for transfers between devices  98.3 us (50%)
  blocking collectives  54.1 us (27%)
  between operations  13.4 us (7%)
  matrix products  13 us (7%)
  local copies, waits for them, and re-layouts  10.2 us (5%)
  starting transfers between devices  4.68 us (2%)
  other arithmetic  3.19 us (2%)
    psum x1, waiting for transfers between devices, local(): totals, numerators = lax.psum((totals, numerators), 'context')  34 us
    reduce_scatter x1, waiting for transfers between devices, local(): lax.psum_scatter(jnp.dot(attention, out_weight, preferred_element_type=jn...  30.2 us
    all_to_all x1, blocking collectives, local(): lax.all_to_all(outgoing, 'expert', split_axis=0, concat_axis=0, tiled=True)  26.2 us
    reduce_scatter x1, waiting for transfers between devices, local(): lax.psum_scatter(partial_out.astype(jnp.bfloat16), 'context', scatter_dim...  25.1 us
    pmax x1, blocking collectives, local(): lax.pmax(local_maximum(page_scores, fresh_scores, row_start), 'context')  11.4 us
    all_to_all x1, waiting for transfers between devices, local(): lax.all_to_all(summed, 'expert', split_axis=0, concat_axis=0, tiled=True)  8.94 us
    all_gather x1, blocking collectives, local(): full_rows = lax.all_gather(hidden_state, 'context', axis=1, tiled=True)  8.45 us
    psum x1, blocking collectives, local(): totals, numerators = lax.psum((totals, numerators), 'context')  8.05 us
  transfers between devices with their start and end apart: 4, of which 4 were waited for; matrix products, arithmetic and copies ran while one was open for 1% of the time, Pallas kernels for 0%

commit v1 on v0

v1 whole, which is shorter than its diff:
```python
import functools

import jax
import jax.numpy as jnp
from jax import lax
from jax.experimental import pallas as pl
from jax.experimental.pallas import tpu as pltpu
from jax.sharding import PartitionSpec as P

LAT = 512
ROPE = 64
QK = 128
VD = 128
NEG = -(2.0**100)
EPS = 1e-06
F32 = jnp.float32
BF16 = jnp.bfloat16
MESH = pl.DeviceIdType.MESH
STAT = 128


def iota(shape, dim):
    return lax.broadcasted_iota(jnp.int32, shape, dim)


def dot(a, b):
    return jnp.dot(a, b, preferred_element_type=F32)


def dot_t(a, b):
    return lax.dot_general(a, b, (((1,), (1,)), ((), ())), preferred_element_type=F32)


def spread(per_leaf, advance):
    leaves, n = per_leaf.shape
    return jnp.broadcast_to(per_leaf[:, None, :], (leaves, advance, n)).reshape(leaves * advance, n)


def masks(c, pt_ref, cl_ref, tp_ref, pool_keys, page_len, fresh_cols, own_leaves):
    leaves, slots = pt_ref.shape
    advance = tp_ref.shape[1]
    rows = leaves * advance
    lengths = jnp.sum(
        jnp.where(
            iota((leaves, leaves), 0) == iota((leaves, leaves), 1),
            jnp.broadcast_to(cl_ref[...].astype(F32), (leaves, leaves)),
            0.0,
        ),
        axis=1,
        keepdims=True,
    )
    remain = lengths - (iota((leaves, slots), 1) * page_len).astype(F32)
    table = pt_ref[...]
    lane = iota((leaves, pool_keys), 1)
    limit = jnp.zeros((leaves, pool_keys), F32)
    pages = pool_keys // page_len
    for p in range(pages):
        here = jnp.sum(jnp.where(table == c * pages + p, remain, 0.0), axis=1, keepdims=True)
        limit = jnp.where(lane // page_len == p, here, limit)
    limit = spread(limit, advance)
    pool_mask = (iota((rows, pool_keys), 1) % page_len).astype(F32) < limit
    token = iota((leaves, fresh_cols), 1) % advance
    parents = tp_ref[...]
    chains = [jnp.where(token == 0, 1.0, 0.0)]
    for t in range(1, advance):
        chain = jnp.where(token == t, 1.0, 0.0)
        for u in range(t):
            chain = jnp.where(parents[:, t : t + 1] == u, chain + chains[u], chain)
        chains.append(chain)
    row = iota((rows, fresh_cols), 0)
    col = iota((rows, fresh_cols), 1)
    linked = jnp.zeros((rows, fresh_cols), F32)
    for t in range(advance):
        linked = jnp.where(row % advance == t, spread(chains[t], advance), linked)
    own = (row // advance == c * own_leaves + col // advance) & (col < own_leaves * advance)
    fresh_mask = (linked > 0.5) & own
    return pool_mask, fresh_mask


def kernel(
    nctx, nexp, page_len, own_leaves,
    q_ref, kl_ref, vl_ref, pool_ref, fresh_ref, pt_ref, cl_ref, tp_ref, ow_hbm, res_ref, gain_ref, ids_ref,
    rw_ref, g_hbm, u_hbm, d_hbm, out_ref,
    kf, att_send, att_recv, w2, g_v, u_v, d_v, w_all, zf, zs, zr, xg, pf, ps, pr, cs, cr, yf, ys, yr,
    loc, att_ss, att_rs, w2_ss, w2_rs, w_ss, w_rs, wp_ss, wp_rs, z_ss, z_rs, agz_ss, agz_rs, agc_ss, agc_rs,
    agp_ss, agp_rs, p_ss, p_rs, c_ss, c_rs, y_ss, y_rs,
):
    c = lax.axis_index("context")
    e = lax.axis_index("expert")
    k, z = e % 2, e // 2
    nz = nexp // 2
    rows = q_ref.shape[0]
    half_rows = rows // 2
    heads = kl_ref.shape[0]
    row_dev, cols = res_ref.shape
    half = cols // 2
    other = 1 - k

    def ctx(d):
        return ((c // 2 + d // 2) % (nctx // 2)) * 2 + (c + d) % 2

    def dev(cc, zz, kk):
        return (cc, zz * 2 + kk)

    def send(src, dst, ss, rs, to):
        return pltpu.make_async_remote_copy(
            src_ref=src, dst_ref=dst, send_sem=ss, recv_sem=rs, device_id=to, device_id_type=MESH
        )

    def got(dst, ss, rs):
        send(dst, dst, ss, rs, dev(c, z, other)).wait_recv()

    def z_loop(body):
        lax.fori_loop(1, nz, lambda d, carry: (body((z + d) % nz), carry)[1], 0)

    barrier = pltpu.get_barrier_semaphore()
    for d in range(nctx):
        for kk in range(2):
            if d or kk:
                pl.semaphore_signal(
                    barrier, inc=1, device_id=dev(ctx(d), z, (k + kk) % 2), device_id_type=MESH
                )
    z_loop(lambda zp: pl.semaphore_signal(barrier, inc=1, device_id=dev(c, zp, k), device_id_type=MESH))

    local = [
        pltpu.make_async_copy(ow_hbm, w2.at[k], loc.at[0]),
        pltpu.make_async_copy(g_hbm, g_v, loc.at[1]),
        pltpu.make_async_copy(u_hbm, u_v, loc.at[2]),
        pltpu.make_async_copy(d_hbm, d_v, loc.at[3]),
    ]
    for copy in local:
        copy.start()

    lane_w = iota((row_dev, STAT), 1)
    dense = jnp.zeros((row_dev, STAT), F32)
    ids, rw = ids_ref[...], rw_ref[...]
    for t in range(ids.shape[1]):
        dense = jnp.where(lane_w == ids[:, t : t + 1], rw[:, t : t + 1], dense)
    w_all[k, z] = dense

    pool_keys = pool_ref.shape[0]
    fresh_keys = fresh_ref.shape[0]
    fresh_cols = kf.shape[0]
    if fresh_cols != fresh_keys:
        kf[...] = jnp.zeros(kf.shape, BF16)
    kf[0:fresh_keys, :] = fresh_ref[...]
    pool_mask, fresh_mask = masks(
        c, pt_ref, cl_ref, tp_ref, pool_keys, page_len, fresh_cols, own_leaves
    )
    qf = q_ref[...].astype(F32)
    scale = (QK + ROPE) ** (-0.5)
    kp = pool_ref[...]
    kfv = kf[...]
    parts = []
    lane_s = iota((rows, STAT), 1)
    stats = jnp.zeros((rows, STAT), F32)
    for h in range(heads):
        at = h * (QK + ROPE)
        lat = dot(qf[:, at : at + QK].astype(BF16), kl_ref[h]).astype(BF16)
        rot = qf[:, at + QK : at + QK + ROPE].astype(BF16)
        sp = (dot_t(lat, kp[:, :LAT]) + dot_t(rot, kp[:, LAT:])) * scale
        sf = (dot_t(lat, kfv[:, :LAT]) + dot_t(rot, kfv[:, LAT:])) * scale
        sp = jnp.where(pool_mask, sp, NEG)
        sf = jnp.where(fresh_mask, sf, NEG)
        top = jnp.maximum(
            jnp.max(sp, axis=1, keepdims=True), jnp.max(sf, axis=1, keepdims=True)
        )
        top = top.astype(BF16).astype(F32)
        ep, ef = jnp.exp(sp - top), jnp.exp(sf - top)
        total = jnp.sum(ep, axis=1, keepdims=True) + jnp.sum(ef, axis=1, keepdims=True)
        numer = dot(ep.astype(BF16), kp[:, :LAT]) + dot(ef.astype(BF16), kfv[:, :LAT])
        numer = numer / total
        high = numer.astype(BF16)
        low = (numer - high.astype(F32)).astype(BF16)
        parts.append(dot(high, vl_ref[h]) + dot(low, vl_ref[h]))
        t_high = total.astype(BF16).astype(F32)
        for i, value in enumerate((top, t_high, total - t_high)):
            stats = jnp.where(lane_s == 3 * h + i, value, stats)
    width = heads * VD + STAT
    message = jnp.concatenate(parts + [stats], axis=1).reshape(nz, 2, row_dev, width)
    for kk in range(2):
        att_send[kk] = message[:, kk].reshape(half_rows, width).astype(BF16)
    att_recv[c * 2 + k] = att_send[k]

    pl.semaphore_wait(barrier, 2 * nctx - 1 + nz - 1)
    att_copies = []
    for d in range(nctx - 1, -1, -1):
        for kk in range(2):
            if d or kk:
                to = (k + kk) % 2
                att_copies.append(
                    send(att_send.at[to], att_recv.at[c * 2 + k], att_ss.at[2 * d + kk], att_rs.at[c * 2 + k],
                         dev(ctx(d), z, to))
                )
                att_copies[-1].start()
    w2_copy = send(ow_hbm, w2.at[k], w2_ss, w2_rs, dev(c, z, other))
    w2_copy.start()
    z_loop(lambda zp: send(w_all.at[k, z], w_all.at[k, z], w_ss.at[zp], w_rs.at[z], dev(c, zp, k)).start())
    for d in range(nctx):
        for kk in range(2):
            if d or kk:
                slot = ctx(d) * 2 + (k + kk) % 2
                got(att_recv.at[slot], att_ss.at[0], att_rs.at[slot])

    merged = []
    for kk in range(2):
        held = [att_recv[cc * 2 + kk].astype(F32) for cc in range(nctx)]
        for h in range(heads):
            base = heads * VD + 3 * h
            tops = [v[:, base : base + 1] for v in held]
            best = functools.reduce(jnp.maximum, tops)
            shares = [
                (v[:, base + 1 : base + 2] + v[:, base + 2 : base + 3]) * jnp.exp(t - best)
                for v, t in zip(held, tops)
            ]
            whole = functools.reduce(jnp.add, shares)
            mixed = functools.reduce(
                jnp.add, [s * v[:, h * VD : (h + 1) * VD] for s, v in zip(shares, held)]
            )
            merged.append((mixed / whole).astype(BF16))
    local[0].wait()
    got(w2.at[other], w2_ss, w2_rs)
    span = heads
    projected = dot(jnp.concatenate(merged[:span], axis=1), w2[0]) + dot(
        jnp.concatenate(merged[span:], axis=1), w2[1]
    )

    def fold(v):
        v = v.reshape(-1, row_dev, cols)
        return jnp.concatenate([v[:, :, :half], v[:, :, half:]], axis=1)

    folded = fold(projected)
    zf[...] = folded
    zs[...] = folded.astype(BF16)
    z_loop(lambda zp: send(zs.at[zp], zr.at[z], z_ss.at[zp], z_rs.at[z], dev(c, zp, k)).start())
    state = zf[z] + fold(res_ref[...].astype(F32))[0]

    def take(d, acc):
        zp = (z + d) % nz
        got(zr.at[zp], z_ss.at[zp], z_rs.at[zp])
        return acc + zr[zp].astype(F32)

    state = lax.fori_loop(1, nz, take, state)
    hidden = state.astype(BF16)
    xg[c, k, z] = hidden

    def ag_z(zp):
        return send(xg.at[c, k, z], xg.at[c, k, z], agz_ss.at[zp], agz_rs.at[z], dev(c, zp, k))

    def ag_c(d, zp):
        piece = xg.at[c, k, zp]
        return send(piece, piece, agc_ss.at[d, zp], agc_rs.at[c, zp], dev(ctx(d), z, k))

    def ag_p(cc, zp):
        piece = xg.at[cc, k, zp]
        return send(piece, piece, agp_ss.at[cc, zp], agp_rs.at[cc, zp], dev(c, z, other))

    z_loop(lambda zp: ag_z(zp).start())

    def onward(zp):
        for d in range(1, nctx - 1):
            ag_c(d, zp).start()
        ag_p(c, zp).start()

    onward(z)

    def arrived(zp):
        got(xg.at[c, k, zp], agz_ss.at[zp], agz_rs.at[zp])
        onward(zp)

    z_loop(arrived)
    lax.fori_loop(0, nz, lambda zp, carry: (ag_c(nctx - 1, zp).start(), carry)[1], 0)

    z_loop(lambda zp: got(w_all.at[k, zp], w_ss.at[zp], w_rs.at[zp]))
    wp_copy = send(w_all.at[k], w_all.at[k], wp_ss, wp_rs, dev(c, z, other))
    wp_copy.start()

    def relay(d):
        cc = ctx(d)

        def body(zp, carry):
            got(xg.at[cc, k, zp], agc_ss.at[0, zp], agc_rs.at[cc, zp])
            ag_p(cc, zp).start()
            return carry

        lax.fori_loop(0, nz, body, 0)

    local[1].wait()
    local[2].wait()
    acc = [jnp.zeros((rows, 1), F32), jnp.zeros((rows, g_v.shape[1]), F32), jnp.zeros((rows, g_v.shape[1]), F32)]

    def expand(d):
        cc = ctx(d)

        def body(zp, carry):
            got(xg.at[cc, other, zp], agp_ss.at[cc, zp], agp_rs.at[cc, zp])
            return carry

        lax.fori_loop(0, nz, body, 0)
        both = [xg[cc, kk].astype(F32) for kk in (k, other)]
        for i in range(2):
            x = jnp.concatenate(
                [v[:, i * row_dev : (i + 1) * row_dev].reshape(half_rows, half) for v in both], axis=0
            )
            at = pl.ds(pl.multiple_of(cc * cols + i * half, half), half)
            scaled = (x * gain_ref[:, at]).astype(BF16)
            acc[0] = acc[0] + jnp.sum(x * x, axis=1, keepdims=True)
            acc[1] = acc[1] + dot(scaled, g_v[at, :])
            acc[2] = acc[2] + dot(scaled, u_v[at, :])

    relay(1)
    expand(0)
    for d in range(2, nctx):
        relay(d)
        expand(d - 1)
    expand(nctx - 1)

    inverse = lax.rsqrt(acc[0] * (1.0 / (nctx * cols)) + EPS)
    gate, up = acc[1] * inverse, acc[2] * inverse
    got(w_all.at[other], wp_ss, wp_rs)
    weights = jnp.concatenate(
        [w_all[kk].reshape(half_rows, STAT) for kk in (k, other)], axis=0
    )
    weight = jnp.sum(jnp.where(iota((rows, STAT), 1) == e, weights, 0.0), axis=1, keepdims=True)
    active = jnp.where(weight > 0.0, gate / (1.0 + jnp.exp(-gate)) * up, 0.0).astype(BF16)
    local[3].wait()

    def contract(d):
        at = pl.ds(pl.multiple_of(ctx(d) * cols, cols), cols)
        out = dot(active, d_v[:, at]) * weight
        pf[d] = out[:half_rows]
        ps[d] = out[half_rows:].astype(BF16)
        pair(d).start()

    def pair(d):
        return send(ps.at[d], pr.at[d], p_ss.at[d], p_rs.at[d], dev(c, z, other))

    def across(d):
        return send(cs.at[d], cr.at[c], c_ss.at[d], c_rs.at[c], dev(ctx(d), z, k))

    def join(d):
        got(pr.at[d], p_ss.at[d], p_rs.at[d])
        both = pf[d] + pr[d].astype(F32)
        if d:
            cs[d] = both.astype(BF16)
            across(d).start()
        return both

    order = list(range(nctx - 1, -1, -1))
    contract(order[0])
    for before, now in zip(order[:-1], order[1:]):
        contract(now)
        join(before)
    total = join(0)
    for d in range(1, nctx):
        cc = ctx(d)
        got(cr.at[cc], c_ss.at[d], c_rs.at[cc])
        total = total + cr[cc].astype(F32)

    folded = fold(total)
    yf[...] = folded
    ys[...] = folded.astype(BF16)
    z_loop(lambda zp: send(ys.at[zp], yr.at[z], y_ss.at[zp], y_rs.at[z], dev(c, zp, k)).start())
    result = hidden.astype(F32) + yf[z]

    def take_last(d, acc):
        zp = (z + d) % nz
        got(yr.at[zp], y_ss.at[zp], y_rs.at[zp])
        return acc + yr[zp].astype(F32)

    result = lax.fori_loop(1, nz, take_last, result)
    out_ref[...] = jnp.concatenate([result[:row_dev], result[row_dev:]], axis=1).astype(BF16)

    for copy in att_copies:
        copy.wait_send()
    w2_copy.wait_send()
    wp_copy.wait_send()

    def drain_z(zp):
        send(w_all.at[k, z], w_all.at[k, z], w_ss.at[zp], w_rs.at[z], dev(c, zp, k)).wait_send()
        send(zs.at[zp], zr.at[z], z_ss.at[zp], z_rs.at[z], dev(c, zp, k)).wait_send()
        ag_z(zp).wait_send()
        send(ys.at[zp], yr.at[z], y_ss.at[zp], y_rs.at[z], dev(c, zp, k)).wait_send()

    z_loop(drain_z)

    def drain(zp, carry):
        for d in range(nctx):
            if d:
                ag_c(d, zp).wait_send()
            ag_p(ctx(d), zp).wait_send()
        return carry

    lax.fori_loop(0, nz, drain, 0)
    for d in range(nctx):
        pair(d).wait_send()
        if d:
            across(d).wait_send()


def local(
    nctx, nexp,
    queries, key_lift, value_lift, page_pool, fresh_latents, page_table, context_lengths, tree_parents,
    out_weight, residual, norm_gain, expert_ids, route_weights, gate_matrix, up_matrix, down_matrix,
):
    nz = nexp // 2
    rows = queries.shape[0]
    half_rows = rows // 2
    row_dev, cols = residual.shape
    half = cols // 2
    heads = key_lift.shape[0]
    width = heads * VD + STAT
    own_leaves, advance, ckv = fresh_latents.shape
    fresh_cols = -(-own_leaves * advance // 128) * 128
    gate, up, down = gate_matrix[0], up_matrix[0], down_matrix[0]
    dma = pltpu.SemaphoreType.DMA
    vm = pl.BlockSpec(memory_space=pltpu.VMEM)
    hbm = pl.BlockSpec(memory_space=pl.ANY)
    piece = (2 * row_dev, half)
    scratch = [
        pltpu.VMEM((fresh_cols, ckv), BF16),
        pltpu.VMEM((2, half_rows, width), BF16),
        pltpu.VMEM((2 * nctx, half_rows, width), BF16),
        pltpu.VMEM((2,) + out_weight.shape, BF16),
        pltpu.VMEM(gate.shape, BF16),
        pltpu.VMEM(up.shape, BF16),
        pltpu.VMEM(down.shape, BF16),
        pltpu.VMEM((2, nz, row_dev, STAT), F32),
        pltpu.VMEM((nz,) + piece, F32),
        pltpu.VMEM((nz,) + piece, BF16),
        pltpu.VMEM((nz,) + piece, BF16),
        pltpu.VMEM((nctx, 2, nz) + piece, BF16),
        pltpu.VMEM((nctx, half_rows, cols), F32),
        pltpu.VMEM((nctx, half_rows, cols), BF16),
        pltpu.VMEM((nctx, half_rows, cols), BF16),
        pltpu.VMEM((nctx, half_rows, cols), BF16),
        pltpu.VMEM((nctx, half_rows, cols), BF16),
        pltpu.VMEM((nz,) + piece, F32),
        pltpu.VMEM((nz,) + piece, BF16),
        pltpu.VMEM((nz,) + piece, BF16),
        dma((4,)),
        dma((2 * nctx,)), dma((2 * nctx,)),
        dma, dma,
        dma((nz,)), dma((nz,)),
        dma, dma,
        dma((nz,)), dma((nz,)),
        dma((nz,)), dma((nz,)),
        dma((nctx, nz)), dma((nctx, nz)),
        dma((nctx, nz)), dma((nctx, nz)),
        dma((nctx,)), dma((nctx,)),
        dma((nctx,)), dma((nctx,)),
        dma((nz,)), dma((nz,)),
    ]
    return pl.pallas_call(
        functools.partial(kernel, nctx, nexp, page_pool.shape[1], own_leaves),
        out_shape=jax.ShapeDtypeStruct((row_dev, cols), BF16),
        in_specs=[vm] * 8 + [hbm] + [vm] * 4 + [hbm] * 3,
        out_specs=vm,
        scratch_shapes=scratch,
        compiler_params=pltpu.CompilerParams(
            collective_id=0, has_side_effects=True, vmem_limit_bytes=60 * 2**20
        ),
    )(
        queries, key_lift, value_lift, page_pool.reshape(-1, ckv), fresh_latents.reshape(-1, ckv), page_table,
        context_lengths.reshape(1, -1), tree_parents, out_weight, residual, norm_gain.reshape(1, -1),
        expert_ids, route_weights, gate, up, down,
    )


def solution(mesh):
    return jax.shard_map(
        functools.partial(local, mesh.shape["context"], mesh.shape["expert"]),
        mesh=mesh,
        in_specs=(
            P(None, "expert"),
            P("expert", None, None),
            P("expert", None, None),
            P("context", None, None),
            P("context", None, None),
            P(),
            P(),
            P(),
            P("expert", "context"),
            P("expert", "context"),
            P(),
            P("expert", None),
            P("expert", None),
            P("expert", None, "context"),
            P("expert", None, "context"),
            P("expert", "context", None),
        ),
        out_specs=P("expert", "context"),
        check_vma=False,
    )
```

time: 197 us -> 42.9 us (0.22)
  waiting for transfers between devices: 98.3 us -> 0 us
  blocking collectives: 54.1 us -> 0 us
  Pallas kernels: 0 us -> 41.3 us
  between operations: 13.4 us -> 0.01 us
  matrix products: 13 us -> 0 us
  local copies, waits for them, and re-layouts: 10.2 us -> 1.36 us
  starting transfers between devices: 4.68 us -> 0 us
  other arithmetic: 3.19 us -> 0 us
    reduce_scatter x2 -> x0, waiting for transfers between devices: 55.3 us -> none  [the longest x1 30.2 us: local(): lax.psum_scatter(jnp.dot(attention, out_weight, preferred_element_type=jn...]
    pallas_call x0 -> x1, Pallas kernels: none -> 41.3 us  [local(): pl.pallas_call(functools.partial(kernel, nctx, nexp, page_pool.shape[1],...]
    psum x1 -> x0, waiting for transfers between devices: 34 us -> none  [local(): totals, numerators = lax.psum((totals, numerators), 'context')]
    all_to_all x1 -> x0, blocking collectives: 26.2 us -> none  [local(): lax.all_to_all(outgoing, 'expert', split_axis=0, concat_axis=0, tiled=True)]
    dot_general x10 -> x0, matrix products: 13 us -> none  [the longest x1 6.33 us: local(): jnp.dot(active, down_matrix[0], preferred_element_type=jnp.float32)]
    pmax x1 -> x0, blocking collectives: 11.4 us -> none  [local(): lax.pmax(local_maximum(page_scores, fresh_scores, row_start), 'context')]
    all_to_all x1 -> x0, waiting for transfers between devices: 8.94 us -> none  [local(): lax.all_to_all(summed, 'expert', split_axis=0, concat_axis=0, tiled=True)]
    all_gather x1 -> x0, blocking collectives: 8.45 us -> none  [local(): full_rows = lax.all_gather(hidden_state, 'context', axis=1, tiled=True)]
  transfers between devices with their start and end apart: 4 -> 0, of which waited for: 4 -> 0; matrix products, arithmetic and copies ran while one was open for 1% -> 0% of each run, Pallas kernels for 0% -> 0%
where the time goes in v1:
time: 42.9 us; the launch traced here: 42.7 us
  Pallas kernels  41.3 us (96%)
  local copies, waits for them, and re-layouts  1.36 us (3%)
    pallas_call x1, Pallas kernels, local(): pl.pallas_call(functools.partial(kernel, nctx, nexp, page_pool.shape[1],...  41.3 us
    unnamed x1, local copies, waits for them, and re-layouts  1.36 us

profile of v1, /device:TPU:0, one launch (start us, length us, event | category | flops | bytes accessed | tf_op | source)
XLA Modules:
  0.0 42.7 jit_solution(4801471045827140324)
XLA Ops:
  0.0 41.3 %shard_map.154 = bf16[8,1792]{1,0:T(8,128)(2,1)} custom-call(bf16[64,384]{1,0:T(8,128)(2,1)} %q_ref.1, bf16[2,128,512]{2,1,0:T(8,128)(2,1)} %kl_ref.1, bf16[2,512,128]{2,1,0:T(8,128)(2,1)} %vl_ref.1, bf16[256,576]{1,0:T(8,128)(2,1)} %bitcast.10, bf16[16,576]{1,0:T(8,128)(2,1)} %bitcast.12, s32[8,12]{1,0:T(8,128)} %pt_ref.1, s32[1,8]{1,0:T(1,128)} %bitcast.13, ...), custom_call_target="tpu_custom_call" | custom-call | tf_op jit(solution)/shard_map/pallas_call | solution.py:454
  41.3 1.4 %copy.18 = bf16[8,1792]{1,0:T(8,128)(2,1)} copy(bf16[8,1792]{1,0:T(8,128)(2,1)} %shard_map.154) | data formatting | bytes 57344
